TPU v7x, 256 devices: a whole 4x4x8 slice. The times are simulated.
256 devices in a mesh: section: 8 (over y, core), dp: 32 (over z, x).
Axes of the slice: x: 4, y: 4, z: 8, core: 2. Of those that a mesh axis runs over, the one named last changes fastest.
Arguments:
- layer_inputs: bfloat16 [8, 15360, 8192], P('section', 'dp')
- key_cotangent: bfloat16 [8, 15360, 512], P('section', 'dp')
- token_counts: int32 [32, 4], P('dp'), may hold values from 30 to 120, as said below
- rollback_flags: int32 [8], replicated, may hold values from 0 to 1
- master_param: float32 [8, 8192, 512], P('section', 'dp'), may hold values from -6 to 6
- first_moment: float32 [8, 8192, 512], P('section', 'dp'), may hold values from -4 to 4
- second_moment: float32 [8, 8192, 512], P('section', 'dp'), may hold values from 0.05 to 1
Outputs:
- new_param: float32 [8, 8192, 512], P('section', 'dp')
- new_first: float32 [8, 8192, 512], P('section', 'dp')
- new_second: float32 [8, 8192, 512], P('section', 'dp')
- update_direction: float32 [8, 8192, 512], P('section', 'dp')
Inputs may be any that keep to these rules, and one draw needn't show every extreme that they name: `token_counts`: each entry counts the leading token slots of its micro-batch that hold tokens; some micro-batch holds 120.
All inputs are finite; a program needn't handle non-finite values.
Results may differ from a plain program's by a relative error of at most 0.00095.
Values may be sent and summed in bfloat16 or wider, within the bound.
A program may use at most 128 MiB of HBM per device.

v0:
```python
import math

import jax
import jax.numpy as jnp
from jax import lax
from jax.sharding import PartitionSpec as P

beta_first = 0.9
beta_second = 0.95
adam_epsilon = 1e-08
weight_decay = 0.1
learn_rate = 0.00015
clip_level = 1.0


def entering(part, axis, combine, identity):
    place = lax.axis_index(axis)
    gathered = lax.all_gather(part, axis)
    state = jnp.zeros_like(part) + jnp.asarray(identity, part.dtype)

    def one(hop, state):
        return combine(state, lax.dynamic_index_in_dim(gathered, hop, 0, False))

    return lax.fori_loop(0, place, one, state)


def broadcast(block, axis, holder):
    block = jnp.where(lax.axis_index(axis) == holder, block, jnp.zeros_like(block))
    return lax.psum(block, axis)


def mask_rows(cotangent, counts_row):
    micro = counts_row.shape[0]
    per_micro = cotangent.shape[0] // micro
    width = cotangent.shape[1]
    shaped = cotangent.reshape(micro, per_micro, width)
    slot_pos = lax.broadcasted_iota(jnp.int32, (micro, per_micro), 1)
    valid = slot_pos < counts_row[:, None]
    return jnp.where(valid[:, :, None], shaped, jnp.zeros((), cotangent.dtype)).reshape(
        micro * per_micro, width
    )


def local(
    layer_inputs,
    key_cotangent,
    token_counts,
    rollback_flags,
    master_param,
    first_moment,
    second_moment,
):
    inputs_local = layer_inputs[0]
    masked = mask_rows(key_cotangent[0], token_counts[0])
    shard_rows = master_param.shape[1]
    width = master_param.shape[2]
    gradient = lax.psum_scatter(
        lax.dot_general(
            inputs_local, masked, (((0,), (0,)), ((), ())), preferred_element_type=jnp.float32
        ),
        "dp",
        scatter_dimension=0,
        tiled=True,
    )
    local_sq = jnp.sum(gradient * gradient)
    section_sq = lax.psum(local_sq, "dp")
    before = entering(
        section_sq, "section", lambda earlier, later: earlier + later, jnp.float32(0.0)
    )
    total_sq = broadcast(before + section_sq, "section", lax.axis_size("section") - 1)
    entries = lax.axis_size("section") * lax.axis_size("dp") * shard_rows * width
    clip_scale = clip_level * math.sqrt(entries) / (jnp.sqrt(total_sq) + 1e-06)
    clipped = gradient * clip_scale
    step_count = (1 + jnp.sum((rollback_flags == 0).astype(jnp.int32))).astype(jnp.float32)
    bias_one = 1.0 - jnp.power(jnp.float32(beta_first), step_count)
    bias_two = 1.0 - jnp.power(jnp.float32(beta_second), step_count)
    param_now = master_param[0]
    new_first = beta_first * first_moment[0] + (1.0 - beta_first) * clipped
    new_second = beta_second * second_moment[0] + (1.0 - beta_second) * clipped * clipped
    update_direction = (
        new_first / bias_one / (jnp.sqrt(new_second / bias_two) + adam_epsilon)
        + weight_decay * param_now
    )
    new_param = param_now - learn_rate * update_direction
    return (new_param[None], new_first[None], new_second[None], update_direction[None])


def solution(mesh):
    placed = (
        P("section", "dp", None),
        P("section", "dp", None),
        P("dp", None),
        P(),
        P("section", "dp", None),
        P("section", "dp", None),
        P("section", "dp", None),
    )
    return jax.shard_map(
        local,
        mesh=mesh,
        in_specs=placed,
        out_specs=(
            P("section", "dp", None),
            P("section", "dp", None),
            P("section", "dp", None),
            P("section", "dp", None),
        ),
        check_vma=False,
    )
```

profile of v0, /device:TPU:1, one launch (start us, length us, event | category | flops | bytes accessed | tf_op | source)
XLA Modules:
  0.0 395.9 jit_solution(3175629560116299076)
XLA Ops:
  7.2 0.0 reduce-scatter.2.cloned.1.call-start
  7.2 0.7 iota_compare_fusion
  7.9 0.1 lt.27
  8.0 13.8 %convolution_bitcast_fusion = f32[8192,512]{0,1:T(8,128)} fusion(bf16[1,480,8192]{2,1,0:T(8,128)(2,1)} %param.9, bf16[1,480,512]{2,1,0:T(8,128)(2,1)} %param.10, pred[480]{0:T(512)(128)(4,1)S(1)} %lt.27), kind=kOutput, calls=%fused_computation | convolution fusion | flops 4026777600 | bytes 25133536 | tf_op jit(solution)/shard_map/dot_general | solution.py:58
  21.8 0.0 copy-start.3
  21.8 0.0 copy-start
  21.8 0.0 copy-start.1
  21.8 0.0 copy-start.2
  21.8 0.0 reduce-scatter.2.cloned.1.call-update
  21.9 0.6 copy-done.3
  22.5 0.6 fusion.10
  23.8 0.0 copy-done
  23.8 0.2 copy.11
  24.1 0.0 copy-done.1
  24.1 0.2 copy.12
  24.3 243.4 %reduce-scatter.2.cloned.1.call-done = f32[256,512]{0,1:T(8,128)} async-done(((f32[8192,512]{0,1:T(8,128)}), f32[256,512]{0,1:T(8,128)}) %reduce-scatter.2.cloned.1.call-update) | async-done | bytes 524304 | tf_op jit(solution)/shard_map/reduce_scatter | solution.py:57
  267.6 1.8 multiply_reduce_fusion
  269.4 0.0 copy-done.4
  269.4 0.7 dynamic-slice
  270.1 59.1 %psum.14 = f32[]{:T(128)} all-reduce(f32[]{:T(128)} %multiply_reduce_fusion), channel_id=1, replica_groups=mesh['section'=8,'dp'=32] {'dp'}, use_global_device_ids=true, to_apply=%region_2.3 | all-reduce | flops 1 | bytes 8 | tf_op jit(solution)/shard_map/psum | solution.py:66
  329.2 1.4 dynamic-update-slice
  330.6 30.0 %all-reduce = f32[8]{0:T(128)S(1)} all-reduce(f32[8]{0:T(128)S(1)} %dynamic-update-slice), channel_id=1, replica_groups=mesh['section'=8,'dp'=32] {'section'}, use_global_device_ids=true, to_apply=%add | all-reduce | flops 8 | bytes 64
  360.7 1.4 while.10
  360.7 0.7 dynamic_slice.5
  362.7 0.0 copy-done.2
  362.7 0.2 copy.13
  362.9 18.1 %psum.15 = f32[]{:T(128)} all-reduce(f32[]{:T(128)S(6)} %select_n.18), channel_id=1, replica_groups=mesh['section'=8,'dp'=32] {'section'}, use_global_device_ids=true, to_apply=%region_5.6 | all-reduce | flops 1 | bytes 8 | tf_op jit(solution)/shard_map/psum | solution.py:29
  381.7 2.3 fusion.3
  384.0 2.0 copy.14
  386.0 1.0 copy.15
  387.0 1.0 copy.16
  388.0 1.0 copy.17
  (2 shorter events, 0.0 us)
Async XLA Ops:
  7.2 260.5 %reduce-scatter.2.cloned.1.call-start = ((), (), s32[]{:S(2)}) async-start(), calls=%async_computation.1 | async-start | bytes 17301504 | tf_op jit(solution)/shard_map/reduce_scatter | solution.py:57
  21.8 0.7 copy-start.3
  21.8 2.0 copy-start
  21.8 2.2 copy-start.1
  21.8 247.6 %copy-start.4 = (u32[256]{0:T(256)S(1)}, u32[256]{0:T(256)}, u32[]{:S(2)}) copy-start(u32[256]{0:T(256)} %constant.53) | copy-start | bytes 3076
  21.8 340.9 %copy-start.2 = (f32[1,256,512]{2,1,0:T(8,128)S(1)}, f32[1,256,512]{2,1,0:T(8,128)}, u32[]{:S(2)}) copy-start(f32[1,256,512]{2,1,0:T(8,128)} %param.15) | copy-start | bytes 1572868
Sparse Core Ops, SparseCore 0:
  22.0 245.5 reduce-scatter.1
where the time goes:
time: 397 us; the launch traced here: 396 us
  waiting for transfers between devices  243 us (61%)
  blocking collectives  107 us (27%)
  between operations  16.2 us (4%)
  matrix products  13.8 us (3%)
  local copies, waits for them, and re-layouts  9.09 us (2%)
  other arithmetic  5.4 us (1%)
    reduce_scatter x1, waiting for transfers between devices, local(): lax.psum_scatter(lax.dot_general(inputs_local, masked, (((0,), (0,)), (()...  243 us
    psum x1, blocking collectives, local(): section_sq = lax.psum(local_sq, 'dp')  59.1 us
    unnamed x1, blocking collectives  30 us
    psum x1, blocking collectives, broadcast(): return lax.psum(block, axis)  18.1 us
    dot_general x1, matrix products, local(): lax.dot_general(inputs_local, masked, (((0,), (0,)), ((), ())), preferred...  13.8 us
    unnamed x20, local copies, waits for them, and re-layouts  8.33 us
  transfers between devices with their start and end apart: 1, of which 1 were waited for; matrix products, arithmetic and copies ran while one was open for 0% of the time, Pallas kernels for 0%

commit v1 on v0

v1 whole, which is shorter than its diff:
```python
import math

import jax
import jax.numpy as jnp
from jax import lax
from jax.experimental import pallas as pl
from jax.experimental.pallas import tpu as pltpu
from jax.sharding import PartitionSpec as P

beta_first = 0.9
beta_second = 0.95
adam_epsilon = 1e-08
weight_decay = 0.1
learn_rate = 0.00015
clip_level = 1.0

NX, NZ, NY = 4, 8, 4
MESH = pl.DeviceIdType.MESH
LIMIT = 32767.0
TINY = 1e-33

PIECES = {"A0": (0, 160), "B0": (160, 96), "A1": (256, 144), "B1": (400, 112)}
SIGN = {"A0": 1, "A1": -1, "B0": 1, "B1": -1}
STEP = {"A0": 160, "A1": 144, "B0": 96, "B1": 112}
DZ_ORDER = (4, 3, -3, 2, -2, 1, -1, 0)
DX_ORDER = (2, 1, -1, 0)

ORDER = (
    0, 32, 96, 64, 4, 1, 8, 36, 68, 100, 33, 40, 97, 2, 65, 34,
    112, 72, 104, 80, 5, 6, 69, 9, 10, 66, 76, 12, 38, 3, 35, 16,
    42, 73, 44, 84, 37, 81, 11, 48, 41, 88, 98, 7, 113, 13, 14, 101,
    105, 17, 116, 120, 18, 108, 43, 46, 39, 20, 50, 70, 24, 67, 52, 77,
    74, 45, 56, 85, 82, 49, 92, 89, 99, 102, 21, 114, 117, 22, 106, 25,
    109, 121, 26, 124, 19, 15, 28, 51, 54, 47, 53, 78, 58, 75, 57, 86,
    60, 83, 93, 71, 90, 115, 103, 118, 107, 30, 110, 122, 29, 125, 27, 23,
    79, 59, 87, 55, 61, 62, 94, 91, 111, 123, 119, 126, 31, 63, 95, 127,
)


def build_tasks():
    tasks = {}
    for c in ("A0", "A1"):
        sg = SIGN[c]
        for dz in DZ_ORDER:
            tasks[(c, "x", dz, 2 * sg)] = (c, (dz, 2), (), ("x", sg))
            tasks[(c, "x", dz, -sg)] = (c, (dz, -sg), (), ("x", -sg))
            tasks[(c, "x", dz, sg)] = (c, (dz, sg), ((c, "x", dz, 2 * sg),), ("x", sg))
            ins = [(c, "x", dz, sg), (c, "x", dz, -sg)]
            d = dz if dz != 4 else 4 * sg
            out = None
            if d == 0:
                ins += [(c, "z", sg), (c, "z", -sg)]
            else:
                s = 1 if d > 0 else -1
                if abs(d) < (4 if s == sg else 3):
                    ins.append((c, "z", d + s))
                out = ("z", s)
            tasks[(c, "z", d)] = (c, (dz, 0), tuple(ins), out)
    for c in ("B0", "B1"):
        sg = SIGN[c]
        for dx in DX_ORDER:
            for k in (4, 3, 2, 1):
                d = k * sg
                ins = () if k == 4 else ((c, "z", dx, d + sg),)
                tasks[(c, "z", dx, d)] = (c, (4 if k == 4 else d, dx), ins, ("z", sg))
            for k in (3, 2, 1):
                d = -k * sg
                ins = () if k == 3 else ((c, "z", dx, d - sg),)
                tasks[(c, "z", dx, d)] = (c, (d, dx), ins, ("z", -sg))
            ins = [(c, "z", dx, sg), (c, "z", dx, -sg)]
            out, d = None, dx
            if dx == 0:
                ins += [(c, "x", sg), (c, "x", -sg)]
            elif dx == 2:
                out, d = ("x", sg), 2 * sg
            elif dx == sg:
                ins.append((c, "x", 2 * sg))
                out = ("x", sg)
            else:
                out = ("x", -sg)
            tasks[(c, "x", d)] = (c, (0, dx), tuple(ins), out)
    return tasks


TASKS = build_tasks()
NAMES = list(TASKS)
SEQUENCE = [NAMES[i] for i in ORDER]
BLOCKS = list(dict.fromkeys(TASKS[n][1] for n in SEQUENCE))
MESSAGES = {}
for _n in SEQUENCE:
    if TASKS[_n][3] is not None:
        _c = TASKS[_n][0]
        MESSAGES[_n] = (_c, sum(1 for m in MESSAGES if MESSAGES[m][0] == _c))
N_MSG = 31
CLASSES = ("A0", "A1", "B0", "B1")
GROUP = 4


def kernel(x_hbm, m_hbm, counts, g_out, sq_out, xbuf, mbuf, masked, mt, part, tmp, grad, *rest):
    snd, rcv, hsnd, hrcv = rest[0:4], rest[4:8], rest[8:12], rest[12:16]
    ssem, rsem, hssem, hrsem, xsem, msem, red, redr0, redr1, s0, r0, s1, r1 = rest[16:]
    width = mbuf.shape[1]
    section, dp = lax.axis_index("section"), lax.axis_index("dp")
    y, core = section // 2, lax.rem(section, 2)
    z, x = dp // NX, lax.rem(dp, NX)

    def at(dz=0, dx=0, dy=0, dc=0):
        return {
            "section": lax.rem(y + dy + NY, NY) * 2 + lax.rem(core + dc, 2),
            "dp": lax.rem(z + dz + NZ, NZ) * NX + lax.rem(x + dx + NX, NX),
        }

    plane = [(0, dx, dy, 0) for dx in range(NX) for dy in range(NY) if (dx, dy) != (0, 0)]
    column = [(dz, 0, 0, dc) for dz in range(NZ) for dc in range(2) if (dz, dc) != (0, 0)]

    mload = pltpu.make_async_copy(m_hbm.at[0], mbuf, msem)
    mload.start()

    def xload(i):
        dz, dx = BLOCKS[i]
        first = (lax.rem(z + dz + NZ, NZ) * NX + lax.rem(x + dx + NX, NX)) * 256
        return pltpu.make_async_copy(
            x_hbm.at[0, :, pl.ds(pl.multiple_of(first, 256), 256)], xbuf.at[i], xsem.at[i]
        )

    for i in range(len(BLOCKS)):
        xload(i).start()

    barrier = pltpu.get_barrier_semaphore()
    peers = plane + column
    for peer in peers:
        pl.semaphore_signal(barrier, inc=1, device_id=at(*peer), device_id_type=MESH)

    mload.wait()
    per_micro = mbuf.shape[0] // counts.shape[1]
    for j in range(counts.shape[1]):
        rows = lax.broadcasted_iota(jnp.int32, (per_micro, width), 0)
        block = mbuf[j * per_micro : (j + 1) * per_micro, :].astype(jnp.float32)
        masked[j * per_micro : (j + 1) * per_micro, :] = jnp.where(rows < counts[0, j], block, 0.0)
    mt[...] = masked[...].T.astype(jnp.bfloat16)

    done = set()

    def need(block):
        if block in done:
            return
        i = BLOCKS.index(block)
        last = min(i + GROUP, len(BLOCKS))
        for j in range(i, last):
            done.add(BLOCKS[j])
            xload(j).wait()

        def dot(j, _):
            part[j] = jnp.dot(mt[...], xbuf[j], preferred_element_type=jnp.float32)
            return 0

        lax.fori_loop(i, last, dot, 0)

    def send(name):
        c, i = MESSAGES[name]
        axis, s = TASKS[name][3]
        k = CLASSES.index(c)
        to = at(dz=s) if axis == "z" else at(dx=s)
        return (
            pltpu.make_async_remote_copy(
                snd[k].at[i], rcv[k].at[i], ssem.at[k, i], rsem.at[k, i], device_id=to, device_id_type=MESH
            ),
            pltpu.make_async_remote_copy(
                hsnd[k].at[i], hrcv[k].at[i], hssem.at[k, i], hrsem.at[k, i], device_id=to, device_id_type=MESH
            ),
        )

    entered = False
    sums = jnp.zeros((8, 256), jnp.float32)
    for name in SEQUENCE:
        c, block, ins, out = TASKS[name]
        first, rows = PIECES[c]
        k, step = CLASSES.index(c), STEP[c]
        need(block)
        b = BLOCKS.index(block)
        scales = []
        for n in ins:
            data, head = send(n)
            head.wait_recv()
            data.wait_recv()
            scales.append(hrcv[k][MESSAGES[n][1]])

        def value(r, size):
            acc = part[b, pl.ds(first + r, size), :]
            for n, scale in zip(ins, scales):
                acc = acc + rcv[k][MESSAGES[n][1], pl.ds(r, size), :].astype(jnp.float32) * scale
            return acc

        if out is None:

            def final(g, total):
                acc = value(g * step, step)
                grad[pl.ds(first + g * step, step), :] = acc
                return total + jnp.sum((acc * acc).reshape(step // 8, 8, 256), axis=0)

            sums = lax.fori_loop(0, rows // step, final, sums)
            continue

        def high(g, top):
            acc = value(g * step, step)
            if ins:
                tmp[pl.ds(g * step, step), :] = acc
            return jnp.maximum(top, jnp.max(jnp.abs(acc).reshape(step // 8, 8, 256), axis=0))

        top = lax.fori_loop(0, rows // step, high, jnp.full((8, 256), TINY, jnp.float32))
        top = jnp.max(top, axis=0, keepdims=True)
        i = MESSAGES[name][1]
        hsnd[k][i] = top * (1.0 / LIMIT)
        inverse = LIMIT / top

        def narrow(g, _):
            acc = tmp[pl.ds(g * step, step), :] if ins else part[b, pl.ds(first + g * step, step), :]
            snd[k][i, pl.ds(g * step, step), :] = jnp.round(acc * inverse).astype(jnp.int16)
            return 0

        lax.fori_loop(0, rows // step, narrow, 0)
        if not entered:
            pl.semaphore_wait(barrier, len(peers))
            entered = True
        data, head = send(name)
        head.start()
        data.start()

    sums = jnp.sum(sums, axis=0, keepdims=True)
    red[0] = sums[:, :128] + sums[:, 128:]
    for q, (dirs, dst, ss, rs) in enumerate(((plane, redr0, s0, r0), (column, redr1, s1, r1))):
        for j, d in enumerate(dirs):
            pltpu.make_async_remote_copy(
                red.at[q], dst.at[j], ss, rs, device_id=at(*d), device_id_type=MESH
            ).start()
        if q == 0:
            for n in SEQUENCE:
                if TASKS[n][3] is not None:
                    data, head = send(n)
                    head.wait_send()
                    data.wait_send()
            for j in range(0, 256, 128):
                g_out[j : j + 128, :] = grad[:, j : j + 128].T
        whole = pltpu.make_async_remote_copy(dst, dst, ss, rs, device_id=at(*dirs[0]), device_id_type=MESH)
        whole.wait_recv()
        red[q + 1] = red[q] + jnp.sum(dst[...], axis=0)
        whole.wait_send()
    sq_out[...] = jnp.broadcast_to(red[2], (8, 128))


def reduced(layer_inputs, key_cotangent, token_counts):
    _, tokens, depth = layer_inputs.shape
    width = key_cotangent.shape[2]
    anywhere = pl.BlockSpec(memory_space=pl.ANY)
    vmem = pl.BlockSpec(memory_space=pltpu.VMEM)
    pieces = [PIECES[c][1] for c in CLASSES]
    return pl.pallas_call(
        kernel,
        out_shape=(
            jax.ShapeDtypeStruct((256, width), jnp.float32),
            jax.ShapeDtypeStruct((8, 128), jnp.float32),
        ),
        in_specs=[anywhere, anywhere, pl.BlockSpec(memory_space=pltpu.SMEM)],
        out_specs=(vmem, vmem),
        scratch_shapes=[
            pltpu.VMEM((32, tokens, 256), jnp.bfloat16),
            pltpu.VMEM((tokens, width), jnp.bfloat16),
            pltpu.VMEM((tokens, width), jnp.float32),
            pltpu.VMEM((width, tokens), jnp.bfloat16),
            pltpu.VMEM((32, width, 256), jnp.float32),
            pltpu.VMEM((160, 256), jnp.float32),
            pltpu.VMEM((width, 256), jnp.float32),
            *[pltpu.VMEM((N_MSG, r, 256), jnp.int16) for r in pieces],
            *[pltpu.VMEM((N_MSG, r, 256), jnp.int16) for r in pieces],
            *[pltpu.VMEM((N_MSG, 1, 256), jnp.float32) for r in pieces],
            *[pltpu.VMEM((N_MSG, 1, 256), jnp.float32) for r in pieces],
            pltpu.SemaphoreType.DMA((4, N_MSG)),
            pltpu.SemaphoreType.DMA((4, N_MSG)),
            pltpu.SemaphoreType.DMA((4, N_MSG)),
            pltpu.SemaphoreType.DMA((4, N_MSG)),
            pltpu.SemaphoreType.DMA((32,)),
            pltpu.SemaphoreType.DMA,
            pltpu.VMEM((3, 1, 128), jnp.float32),
            pltpu.VMEM((15, 1, 128), jnp.float32),
            pltpu.VMEM((15, 1, 128), jnp.float32),
            pltpu.SemaphoreType.DMA,
            pltpu.SemaphoreType.DMA,
            pltpu.SemaphoreType.DMA,
            pltpu.SemaphoreType.DMA,
        ],
        compiler_params=pltpu.CompilerParams(
            collective_id=0, has_side_effects=True, vmem_limit_bytes=56 << 20
        ),
    )(layer_inputs, key_cotangent, token_counts)


def local(
    layer_inputs,
    key_cotangent,
    token_counts,
    rollback_flags,
    master_param,
    first_moment,
    second_moment,
):
    shard_rows = master_param.shape[1]
    width = master_param.shape[2]
    gradient, squares = reduced(layer_inputs, key_cotangent, token_counts)
    total_sq = jnp.sum(squares[0])
    entries = lax.axis_size("section") * lax.axis_size("dp") * shard_rows * width
    clip_scale = clip_level * math.sqrt(entries) / (jnp.sqrt(total_sq) + 1e-06)
    clipped = gradient * clip_scale
    step_count = (1 + jnp.sum((rollback_flags == 0).astype(jnp.int32))).astype(jnp.float32)
    bias_one = 1.0 - jnp.power(jnp.float32(beta_first), step_count)
    bias_two = 1.0 - jnp.power(jnp.float32(beta_second), step_count)
    param_now = master_param[0]
    new_first = beta_first * first_moment[0] + (1.0 - beta_first) * clipped
    new_second = beta_second * second_moment[0] + (1.0 - beta_second) * clipped * clipped
    update_direction = (
        new_first / bias_one / (jnp.sqrt(new_second / bias_two) + adam_epsilon)
        + weight_decay * param_now
    )
    new_param = param_now - learn_rate * update_direction
    return (new_param[None], new_first[None], new_second[None], update_direction[None])


def solution(mesh):
    placed = (
        P("section", "dp", None),
        P("section", "dp", None),
        P("dp", None),
        P(),
        P("section", "dp", None),
        P("section", "dp", None),
        P("section", "dp", None),
    )
    return jax.shard_map(
        local,
        mesh=mesh,
        in_specs=placed,
        out_specs=(P("section", "dp", None),) * 4,
        check_vma=False,
    )
```

time: 397 us -> 86 us (0.22)
  waiting for transfers between devices: 243 us -> 0 us
  blocking collectives: 107 us -> 0 us
  Pallas kernels: 0 us -> 78.1 us
  between operations: 16.2 us -> 2.16 us
  matrix products: 13.8 us -> 0 us
  local copies, waits for them, and re-layouts: 9.09 us -> 0.01 us
    reduce_scatter x1 -> x0, waiting for transfers between devices: 243 us -> none  [local(): lax.psum_scatter(lax.dot_general(inputs_local, masked, (((0,), (0,)), (()...]
    pallas_call x0 -> x1, Pallas kernels: none -> 78.1 us  [reduced(): pl.pallas_call(kernel, out_shape=(jax.ShapeDtypeStruct((256, width), jnp....]
    psum x2 -> x0, blocking collectives: 77.2 us -> none  [the longest x1 59.1 us: local(): section_sq = lax.psum(local_sq, 'dp')]
    unnamed x1 -> x0, blocking collectives: 30 us -> none
    dot_general x1 -> x0, matrix products: 13.8 us -> none  [local(): lax.dot_general(inputs_local, masked, (((0,), (0,)), ((), ())), preferred...]
    unnamed x20 -> x6, local copies, waits for them, and re-layouts: 8.33 us -> 0.01 us
  transfers between devices with their start and end apart: 1 -> 0, of which waited for: 1 -> 0; matrix products, arithmetic and copies ran while one was open for 0% -> 0% of each run, Pallas kernels for 0% -> 0%
where the time goes in v1:
time: 86 us; the launch traced here: 85.8 us
  Pallas kernels  78.1 us (91%)
  other arithmetic  5.46 us (6%)
  between operations  2.16 us (3%)
    pallas_call x1, Pallas kernels, reduced(): pl.pallas_call(kernel, out_shape=(jax.ShapeDtypeStruct((256, width), jnp....  78.1 us
    broadcast_in_dim x1, other arithmetic, local(): new_param[None]  2.77 us

profile of v1, /device:TPU:1, one launch (start us, length us, event | category | flops | bytes accessed | tf_op | source)
XLA Modules:
  0.0 85.8 jit_solution(8333153656088160097)
XLA Ops:
  0.6 0.0 copy-start.1
  0.6 0.0 copy-start.2
  0.7 0.0 copy-start
  0.7 1.4 %fusion.5 = s32[]{:T(128)} fusion(s32[8]{0:T(128)} %param.10), kind=kLoop, calls=%fused_computation.10 | loop fusion | flops 23 | bytes 36 | tf_op jit(solution)/shard_map/reduce_sum | solution.py:313
  2.8 78.1 %shard_map.102 = (f32[256,512]{1,0:T(8,128)}, f32[8,128]{1,0:T(8,128)}) custom-call(bf16[1,480,8192]{2,1,0:T(8,128)(2,1)} %x_hbm.1, bf16[1,480,512]{2,1,0:T(8,128)(2,1)} %m_hbm.1, s32[1,4]{1,0:T(1,128)} %counts.1), custom_call_target="tpu_custom_call" | custom-call | tf_op jit(solution)/shard_map/pallas_call | solution.py:257
  80.9 1.3 %slice_reduce_fusion = f32[]{:T(128)} fusion(f32[8,128]{1,0:T(8,128)} %get-tuple-element.7), kind=kLoop, calls=%fused_computation.11 | loop fusion | flops 127 | bytes 516 | tf_op jit(solution)/shard_map/reduce_sum | solution.py:309
  83.0 0.0 copy-done.1
  83.0 0.0 copy-done.2
  83.0 0.0 copy-done
  83.0 2.8 %fusion.2 = (f32[1,256,512]{2,1,0:T(8,128)}, f32[256,512]{1,0:T(8,128)}, f32[1,256,512]{2,1,0:T(8,128)}, f32[1,256,512]{2,1,0:T(8,128)}) fusion(f32[1,256,512]{2,1,0:T(8,128)S(1)} %copy-done, f32[]{:T(128)S(6)} %sub.10, f32[1,256,512]{2,1,0:T(8,128)S(1)} %copy-done.1, f32[]{:T(128)S(6)} %sub.9, f32[256,512]{1,0:T(8,128)} %get-tuple-element.6, f32[]{:T(128)S(6)} %div.16, ...), kind=kLoop, calls=%fused_computation.6 | loop fusion | flops 2097152 | bytes 4194316 | tf_op jit(solution)/shard_map/broadcast_in_dim | solution.py:324
Async XLA Ops:
  0.6 82.3 %copy-start.1 = (f32[1,256,512]{2,1,0:T(8,128)S(1)}, f32[1,256,512]{2,1,0:T(8,128)}, u32[]{:S(2)}) copy-start(f32[1,256,512]{2,1,0:T(8,128)} %param.13) | copy-start | bytes 1572868
  0.6 82.3 %copy-start.2 = (f32[1,256,512]{2,1,0:T(8,128)S(1)}, f32[1,256,512]{2,1,0:T(8,128)}, u32[]{:S(2)}) copy-start(f32[1,256,512]{2,1,0:T(8,128)} %param.12) | copy-start | bytes 1572868
  0.7 82.3 %copy-start = (f32[1,256,512]{2,1,0:T(8,128)S(1)}, f32[1,256,512]{2,1,0:T(8,128)}, u32[]{:S(2)}) copy-start(f32[1,256,512]{2,1,0:T(8,128)} %param.11) | copy-start | bytes 1572868

commit v2 on v1

--- a/solution.py
+++ b/solution.py
@@ -1,3 +1,4 @@
+import functools
 import math
 
 import jax
@@ -26,14 +27,14 @@
 DX_ORDER = (2, 1, -1, 0)
 
 ORDER = (
-    0, 32, 96, 64, 4, 1, 8, 36, 68, 100, 33, 40, 97, 2, 65, 34,
-    112, 72, 104, 80, 5, 6, 69, 9, 10, 66, 76, 12, 38, 3, 35, 16,
-    42, 73, 44, 84, 37, 81, 11, 48, 41, 88, 98, 7, 113, 13, 14, 101,
-    105, 17, 116, 120, 18, 108, 43, 46, 39, 20, 50, 70, 24, 67, 52, 77,
-    74, 45, 56, 85, 82, 49, 92, 89, 99, 102, 21, 114, 117, 22, 106, 25,
-    109, 121, 26, 124, 19, 15, 28, 51, 54, 47, 53, 78, 58, 75, 57, 86,
-    60, 83, 93, 71, 90, 115, 103, 118, 107, 30, 110, 122, 29, 125, 27, 23,
-    79, 59, 87, 55, 61, 62, 94, 91, 111, 123, 119, 126, 31, 63, 95, 127,
+    0, 96, 64, 32, 8, 104, 80, 41, 72, 84, 9, 112, 36, 124, 108, 88,
+    68, 12, 120, 40, 17, 81, 49, 100, 16, 1, 76, 105, 97, 4, 65, 69,
+    89, 60, 73, 34, 113, 109, 2, 77, 56, 85, 33, 101, 92, 42, 44, 24,
+    116, 38, 10, 114, 5, 66, 52, 3, 98, 121, 6, 28, 125, 106, 82, 90,
+    37, 102, 48, 45, 115, 35, 18, 110, 46, 117, 13, 11, 14, 99, 67, 26,
+    7, 70, 83, 43, 50, 86, 20, 107, 39, 54, 122, 74, 25, 118, 103, 57,
+    53, 19, 21, 78, 15, 58, 51, 71, 47, 22, 61, 75, 111, 93, 126, 87,
+    62, 27, 91, 119, 123, 55, 30, 29, 59, 94, 79, 23, 127, 63, 31, 95,
 )
 
 
@@ -94,11 +95,12 @@
 N_MSG = 31
 CLASSES = ("A0", "A1", "B0", "B1")
 GROUP = 4
-
-
-def kernel(x_hbm, m_hbm, counts, g_out, sq_out, xbuf, mbuf, masked, mt, part, tmp, grad, *rest):
+STEPS = 4
+
+
+def kernel(entries, x_hbm, m_hbm, counts, flags, g_out, scale_out, xbuf, mbuf, masked, mt, part, tmp, grad, *rest):
     snd, rcv, hsnd, hrcv = rest[0:4], rest[4:8], rest[8:12], rest[12:16]
-    ssem, rsem, hssem, hrsem, xsem, msem, red, redr0, redr1, s0, r0, s1, r1 = rest[16:]
+    ssem, rsem, hssem, hrsem, xsem, msem, red, redr0, redr1, s0, r0, s1, r1, turned, gsem, far, scale = rest[16:]
     width = mbuf.shape[1]
     section, dp = lax.axis_index("section"), lax.axis_index("dp")
     y, core = section // 2, lax.rem(section, 2)
@@ -123,15 +125,17 @@
             x_hbm.at[0, :, pl.ds(pl.multiple_of(first, 256), 256)], xbuf.at[i], xsem.at[i]
         )
 
-    for i in range(len(BLOCKS)):
-        xload(i).start()
+    xload(0).start()
 
     barrier = pltpu.get_barrier_semaphore()
-    peers = plane + column
+    peers = [(1, 0, 0, 0), (-1, 0, 0, 0), (0, 1, 0, 0), (0, -1, 0, 0)]
+    peers += [(0, 0, 1, 0), (0, 0, -1, 0), (0, 0, 0, 1)]
     for peer in peers:
         pl.semaphore_signal(barrier, inc=1, device_id=at(*peer), device_id_type=MESH)
 
     mload.wait()
+    for i in range(1, len(BLOCKS)):
+        xload(i).start()
     per_micro = mbuf.shape[0] // counts.shape[1]
     for j in range(counts.shape[1]):
         rows = lax.broadcasted_iota(jnp.int32, (per_micro, width), 0)
@@ -145,7 +149,7 @@
         if block in done:
             return
         i = BLOCKS.index(block)
-        last = min(i + GROUP, len(BLOCKS))
+        last = min(i + (GROUP if i >= GROUP else 1), len(BLOCKS))
         for j in range(i, last):
             done.add(BLOCKS[j])
             xload(j).wait()
@@ -172,8 +176,10 @@
 
     entered = False
     sums = jnp.zeros((8, 256), jnp.float32)
-    for name in SEQUENCE:
+    for place, name in enumerate(SEQUENCE):
         c, block, ins, out = TASKS[name]
+        if place == 24:
+            pl.semaphore_wait(far, 1)
         first, rows = PIECES[c]
         k, step = CLASSES.index(c), STEP[c]
         need(block)
@@ -221,6 +227,7 @@
         lax.fori_loop(0, rows // step, narrow, 0)
         if not entered:
             pl.semaphore_wait(barrier, len(peers))
+            pl.semaphore_signal(far, inc=1, device_id=at(0, 0, 1, 0), device_id_type=MESH)
             entered = True
         data, head = send(name)
         head.start()
@@ -240,28 +247,44 @@
                     head.wait_send()
                     data.wait_send()
             for j in range(0, 256, 128):
-                g_out[j : j + 128, :] = grad[:, j : j + 128].T
+                turned[j : j + 128, :] = grad[:, j : j + 128].T
+            store = pltpu.make_async_copy(turned, g_out, gsem)
+            store.start()
         whole = pltpu.make_async_remote_copy(dst, dst, ss, rs, device_id=at(*dirs[0]), device_id_type=MESH)
         whole.wait_recv()
         red[q + 1] = red[q] + jnp.sum(dst[...], axis=0)
         whole.wait_send()
-    sq_out[...] = jnp.broadcast_to(red[2], (8, 128))
-
-
-def reduced(layer_inputs, key_cotangent, token_counts):
+    total_sq = jnp.sum(red[2], axis=1, keepdims=True)
+    clip_scale = clip_level * math.sqrt(entries) / (jnp.sqrt(total_sq) + 1e-06)
+    power_one, power_two = jnp.float32(beta_first), jnp.float32(beta_second)
+    for i in range(flags.shape[0]):
+        counted = flags[i] == 0
+        power_one = power_one * jnp.where(counted, jnp.float32(beta_first), jnp.float32(1.0))
+        power_two = power_two * jnp.where(counted, jnp.float32(beta_second), jnp.float32(1.0))
+    shape = (1, width)
+    scale[0:1, :] = jnp.broadcast_to(clip_scale, shape)
+    scale[1:2, :] = 1.0 / (1.0 - jnp.full(shape, power_one, jnp.float32))
+    scale[2:3, :] = 1.0 / (1.0 - jnp.full(shape, power_two, jnp.float32))
+    scale[3:8, :] = jnp.zeros((5, width), jnp.float32)
+    put = pltpu.make_async_copy(scale, scale_out, msem)
+    put.start()
+    put.wait()
+    store.wait()
+
+
+def reduced(layer_inputs, key_cotangent, token_counts, flags, entries):
     _, tokens, depth = layer_inputs.shape
     width = key_cotangent.shape[2]
-    anywhere = pl.BlockSpec(memory_space=pl.ANY)
-    vmem = pl.BlockSpec(memory_space=pltpu.VMEM)
+    anywhere = pl.BlockSpec(memory_space=pltpu.HBM)
     pieces = [PIECES[c][1] for c in CLASSES]
     return pl.pallas_call(
-        kernel,
+        functools.partial(kernel, entries),
         out_shape=(
             jax.ShapeDtypeStruct((256, width), jnp.float32),
-            jax.ShapeDtypeStruct((8, 128), jnp.float32),
+            jax.ShapeDtypeStruct((8, width), jnp.float32),
         ),
-        in_specs=[anywhere, anywhere, pl.BlockSpec(memory_space=pltpu.SMEM)],
-        out_specs=(vmem, vmem),
+        in_specs=[anywhere, anywhere, *[pl.BlockSpec(memory_space=pltpu.SMEM)] * 2],
+        out_specs=(anywhere, anywhere),
         scratch_shapes=[
             pltpu.VMEM((32, tokens, 256), jnp.bfloat16),
             pltpu.VMEM((tokens, width), jnp.bfloat16),
@@ -287,11 +310,48 @@
             pltpu.SemaphoreType.DMA,
             pltpu.SemaphoreType.DMA,
             pltpu.SemaphoreType.DMA,
+            pltpu.VMEM((256, width), jnp.float32),
+            pltpu.SemaphoreType.DMA,
+            pltpu.SemaphoreType.REGULAR,
+            pltpu.VMEM((8, width), jnp.float32),
         ],
         compiler_params=pltpu.CompilerParams(
             collective_id=0, has_side_effects=True, vmem_limit_bytes=56 << 20
         ),
-    )(layer_inputs, key_cotangent, token_counts)
+    )(layer_inputs, key_cotangent, token_counts, flags)
+
+
+def update(grad, scale_hbm, param, first, second, *rest):
+    outs, held, bufs, scale, gsem, sems, ssem = rest[:4], rest[4:8], rest[8:12], *rest[12:]
+    step = bufs[0].shape[0] // STEPS
+    get = pltpu.make_async_copy(scale_hbm, scale, ssem)
+    get.start()
+    loads = []
+    for i in range(STEPS):
+        part = pl.ds(i * step, step)
+        sources = (grad.at[part], param.at[0, part], first.at[0, part], second.at[0, part])
+        loads.append([])
+        for j, source in enumerate(sources):
+            loads[i].append(pltpu.make_async_copy(source, held[j].at[part], gsem.at[j, i]))
+            loads[i][j].start()
+    get.wait()
+    unbias_one, unbias_two = scale[1:2, :], scale[2:3, :]
+    stores = []
+    for i in range(STEPS):
+        part = pl.ds(i * step, step)
+        for load in loads[i]:
+            load.wait()
+        clipped = held[0][part, :] * scale[0:1, :]
+        now = held[1][part, :]
+        one = beta_first * held[2][part, :] + (1.0 - beta_first) * clipped
+        two = beta_second * held[3][part, :] + (1.0 - beta_second) * clipped * clipped
+        turn = one * unbias_one / (jnp.sqrt(two * unbias_two) + adam_epsilon) + weight_decay * now
+        for j, value in enumerate((now - learn_rate * turn, one, two, turn)):
+            bufs[j][part, :] = value
+            stores.append(pltpu.make_async_copy(bufs[j].at[part], outs[j].at[0, part], sems.at[j, i]))
+            stores[-1].start()
+    for store in stores:
+        store.wait()
 
 
 def local(
@@ -303,25 +363,25 @@
     first_moment,
     second_moment,
 ):
-    shard_rows = master_param.shape[1]
-    width = master_param.shape[2]
-    gradient, squares = reduced(layer_inputs, key_cotangent, token_counts)
-    total_sq = jnp.sum(squares[0])
+    _, shard_rows, width = master_param.shape
     entries = lax.axis_size("section") * lax.axis_size("dp") * shard_rows * width
-    clip_scale = clip_level * math.sqrt(entries) / (jnp.sqrt(total_sq) + 1e-06)
-    clipped = gradient * clip_scale
-    step_count = (1 + jnp.sum((rollback_flags == 0).astype(jnp.int32))).astype(jnp.float32)
-    bias_one = 1.0 - jnp.power(jnp.float32(beta_first), step_count)
-    bias_two = 1.0 - jnp.power(jnp.float32(beta_second), step_count)
-    param_now = master_param[0]
-    new_first = beta_first * first_moment[0] + (1.0 - beta_first) * clipped
-    new_second = beta_second * second_moment[0] + (1.0 - beta_second) * clipped * clipped
-    update_direction = (
-        new_first / bias_one / (jnp.sqrt(new_second / bias_two) + adam_epsilon)
-        + weight_decay * param_now
-    )
-    new_param = param_now - learn_rate * update_direction
-    return (new_param[None], new_first[None], new_second[None], update_direction[None])
+    gradient, scale = reduced(layer_inputs, key_cotangent, token_counts, rollback_flags, entries)
+    anywhere = pl.BlockSpec(memory_space=pltpu.HBM)
+    return pl.pallas_call(
+        update,
+        out_shape=(jax.ShapeDtypeStruct(master_param.shape, jnp.float32),) * 4,
+        in_specs=(anywhere,) * 5,
+        out_specs=(anywhere,) * 4,
+        scratch_shapes=[
+            *[pltpu.VMEM((shard_rows, width), jnp.float32)] * 8,
+            pltpu.VMEM((8, width), jnp.float32),
+            pltpu.SemaphoreType.DMA((4, STEPS)),
+            pltpu.SemaphoreType.DMA((4, STEPS)),
+            pltpu.SemaphoreType.DMA,
+        ],
+        compiler_params=pltpu.CompilerParams(vmem_limit_bytes=60 << 20),
+        cost_estimate=pl.CostEstimate(flops=20 << 17, bytes_accessed=4 << 20, transcendentals=1 << 17),
+    )(gradient, scale, master_param, first_moment, second_moment)
 
 
 def solution(mesh):

time: 86 us -> 76 us (0.88)
  other arithmetic: 5.46 us -> 0 us
  Pallas kernels: 78.1 us -> 75.2 us
  between operations: 2.16 us -> 0.64 us
    pallas_call x1 -> x2, Pallas kernels: 78.1 us -> 75.2 us  [the longest x1 72.1 us: reduced(): pl.pallas_call(functools.partial(kernel, entries), out_shape=(jax.ShapeDt...]
    broadcast_in_dim x1 -> x0, other arithmetic: 2.77 us -> none  [local(): new_param[None]]
    reduce_sum x2 -> x0, other arithmetic: 2.69 us -> none  [the longest x1 1.41 us: local(): jnp.sum((rollback_flags == 0).astype(jnp.int32))]
where the time goes in v2:
time: 76 us; the launch traced here: 75.8 us
  Pallas kernels  75.2 us (99%)
    pallas_call x1, Pallas kernels, reduced(): pl.pallas_call(functools.partial(kernel, entries), out_shape=(jax.ShapeDt...  72.1 us
    pallas_call x1, Pallas kernels, local(): pl.pallas_call(update, out_shape=(jax.ShapeDtypeStruct(master_param.shape...  3.11 us

profile of v2, /device:TPU:1, one launch (start us, length us, event | category | flops | bytes accessed | tf_op | source)
XLA Modules:
  0.0 75.8 jit_solution(12600365652927351514)
XLA Ops:
  0.6 72.1 %shard_map.102 = (f32[256,512]{1,0:T(8,128)}, f32[8,512]{1,0:T(8,128)}) custom-call(bf16[1,480,8192]{2,1,0:T(8,128)(2,1)} %x_hbm.1, bf16[1,480,512]{2,1,0:T(8,128)(2,1)} %m_hbm.1, s32[1,4]{1,0:T(1,128)} %counts.1, s32[8]{0:T(128)} %flags.1), custom_call_target="tpu_custom_call" | custom-call | tf_op jit(solution)/shard_map/pallas_call | solution.py:280
  72.7 3.1 %shard_map.103 = (f32[1,256,512]{2,1,0:T(8,128)}, f32[1,256,512]{2,1,0:T(8,128)}, f32[1,256,512]{2,1,0:T(8,128)}, f32[1,256,512]{2,1,0:T(8,128)}) custom-call(f32[256,512]{1,0:T(8,128)} %get-tuple-element.6.grad, f32[8,512]{1,0:T(8,128)} %get-tuple-element.7.scale_hbm, f32[1,256,512]{2,1,0:T(8,128)} %param.15, f32[1,256,512]{2,1,0:T(8,128)} %first.1, ...), custom_call_target="tpu_custom_call" | custom-call | flops 2621440 | bytes 4194304 | tf_op jit(solution)/shard_map/pallas_call | solution.py:370

commit v3 on v2

--- a/solution.py
+++ b/solution.py
@@ -92,15 +92,18 @@
     if TASKS[_n][3] is not None:
         _c = TASKS[_n][0]
         MESSAGES[_n] = (_c, sum(1 for m in MESSAGES if MESSAGES[m][0] == _c))
+TAKERS = [n for n in SEQUENCE if TASKS[n][2]]
+TAKER = {m: i for i, n in enumerate(TAKERS) for m in TASKS[n][2]}
 N_MSG = 31
 CLASSES = ("A0", "A1", "B0", "B1")
+LANES = 128
 GROUP = 4
 STEPS = 4
 
 
-def kernel(entries, x_hbm, m_hbm, counts, flags, g_out, scale_out, xbuf, mbuf, masked, mt, part, tmp, grad, *rest):
+def kernel(entries, x_hbm, m_hbm, counts_hbm, flags_hbm, g_out, scale_out, xbuf, mbuf, masked, mt, part, tmp, grad, *rest):
     snd, rcv, hsnd, hrcv = rest[0:4], rest[4:8], rest[8:12], rest[12:16]
-    ssem, rsem, hssem, hrsem, xsem, msem, red, redr0, redr1, s0, r0, s1, r1, turned, gsem, far, scale = rest[16:]
+    ssem, rsem, hssem, dummy, xsem, msem, red, redr0, redr1, s0, r0, s1, r1, turned, gsem, far, scale, counts, flags, csem, fsem = rest[16:]
     width = mbuf.shape[1]
     section, dp = lax.axis_index("section"), lax.axis_index("dp")
     y, core = section // 2, lax.rem(section, 2)
@@ -117,12 +120,14 @@
 
     mload = pltpu.make_async_copy(m_hbm.at[0], mbuf, msem)
     mload.start()
+    cload = pltpu.make_async_copy(counts_hbm, counts, csem)
+    cload.start()
 
     def xload(i):
         dz, dx = BLOCKS[i]
         first = (lax.rem(z + dz + NZ, NZ) * NX + lax.rem(x + dx + NX, NX)) * 256
         return pltpu.make_async_copy(
-            x_hbm.at[0, :, pl.ds(pl.multiple_of(first, 256), 256)], xbuf.at[i], xsem.at[i]
+            x_hbm.at[0, :, pl.ds(pl.multiple_of(first, 256), 256)], xbuf.at[i], xsem.at[0 if i == 0 else i // GROUP + 1]
         )
 
     xload(0).start()
@@ -133,6 +138,9 @@
     for peer in peers:
         pl.semaphore_signal(barrier, inc=1, device_id=at(*peer), device_id_type=MESH)
 
+    fload = pltpu.make_async_copy(flags_hbm, flags, fsem)
+    fload.start()
+    cload.wait()
     mload.wait()
     for i in range(1, len(BLOCKS)):
         xload(i).start()
@@ -149,10 +157,10 @@
         if block in done:
             return
         i = BLOCKS.index(block)
-        last = min(i + (GROUP if i >= GROUP else 1), len(BLOCKS))
-        for j in range(i, last):
-            done.add(BLOCKS[j])
-            xload(j).wait()
+        last = 1 if i == 0 else (i // GROUP + 1) * GROUP
+        done.update(BLOCKS[i:last])
+        group = xbuf.at[pl.ds(i, last - i)]
+        pltpu.make_async_copy(group, group, xsem.at[0 if i == 0 else i // GROUP + 1]).wait()
 
         def dot(j, _):
             part[j] = jnp.dot(mt[...], xbuf[j], preferred_element_type=jnp.float32)
@@ -167,10 +175,10 @@
         to = at(dz=s) if axis == "z" else at(dx=s)
         return (
             pltpu.make_async_remote_copy(
-                snd[k].at[i], rcv[k].at[i], ssem.at[k, i], rsem.at[k, i], device_id=to, device_id_type=MESH
+                snd[k].at[i], rcv[k].at[i], ssem.at[k], rsem.at[TAKER[name]], device_id=to, device_id_type=MESH
             ),
             pltpu.make_async_remote_copy(
-                hsnd[k].at[i], hrcv[k].at[i], hssem.at[k, i], hrsem.at[k, i], device_id=to, device_id_type=MESH
+                hsnd[k].at[i], hrcv[k].at[i], hssem.at[k], rsem.at[TAKER[name]], device_id=to, device_id_type=MESH
             ),
         )
 
@@ -185,10 +193,12 @@
         need(block)
         b = BLOCKS.index(block)
         scales = []
+        if ins:
+            whole = dummy.at[pl.ds(0, len(ins) * (rows + 2))]
+            pltpu.make_async_remote_copy(
+                whole, whole, ssem.at[k], rsem.at[TAKER[ins[0]]], device_id=at(dx=1), device_id_type=MESH
+            ).wait_recv()
         for n in ins:
-            data, head = send(n)
-            head.wait_recv()
-            data.wait_recv()
             scales.append(hrcv[k][MESSAGES[n][1]])
 
         def value(r, size):
@@ -241,11 +251,11 @@
                 red.at[q], dst.at[j], ss, rs, device_id=at(*d), device_id_type=MESH
             ).start()
         if q == 0:
-            for n in SEQUENCE:
-                if TASKS[n][3] is not None:
-                    data, head = send(n)
-                    head.wait_send()
-                    data.wait_send()
+            for k in range(len(CLASSES)):
+                for buf, sem in ((snd[k], ssem.at[k]), (hsnd[k], hssem.at[k])):
+                    pltpu.make_async_remote_copy(
+                        buf, buf, sem, rsem.at[0], device_id=at(dx=1), device_id_type=MESH
+                    ).wait_send()
             for j in range(0, 256, 128):
                 turned[j : j + 128, :] = grad[:, j : j + 128].T
             store = pltpu.make_async_copy(turned, g_out, gsem)
@@ -256,6 +266,7 @@
         whole.wait_send()
     total_sq = jnp.sum(red[2], axis=1, keepdims=True)
     clip_scale = clip_level * math.sqrt(entries) / (jnp.sqrt(total_sq) + 1e-06)
+    fload.wait()
     power_one, power_two = jnp.float32(beta_first), jnp.float32(beta_second)
     for i in range(flags.shape[0]):
         counted = flags[i] == 0
@@ -283,7 +294,7 @@
             jax.ShapeDtypeStruct((256, width), jnp.float32),
             jax.ShapeDtypeStruct((8, width), jnp.float32),
         ),
-        in_specs=[anywhere, anywhere, *[pl.BlockSpec(memory_space=pltpu.SMEM)] * 2],
+        in_specs=[anywhere] * 4,
         out_specs=(anywhere, anywhere),
         scratch_shapes=[
             pltpu.VMEM((32, tokens, 256), jnp.bfloat16),
@@ -297,11 +308,11 @@
             *[pltpu.VMEM((N_MSG, r, 256), jnp.int16) for r in pieces],
             *[pltpu.VMEM((N_MSG, 1, 256), jnp.float32) for r in pieces],
             *[pltpu.VMEM((N_MSG, 1, 256), jnp.float32) for r in pieces],
-            pltpu.SemaphoreType.DMA((4, N_MSG)),
-            pltpu.SemaphoreType.DMA((4, N_MSG)),
-            pltpu.SemaphoreType.DMA((4, N_MSG)),
-            pltpu.SemaphoreType.DMA((4, N_MSG)),
-            pltpu.SemaphoreType.DMA((32,)),
+            pltpu.SemaphoreType.DMA((len(CLASSES),)),
+            pltpu.SemaphoreType.DMA((len(TAKERS),)),
+            pltpu.SemaphoreType.DMA((len(CLASSES),)),
+            pltpu.VMEM((4 * 162, 1, LANES), jnp.float32),
+            pltpu.SemaphoreType.DMA((len(BLOCKS) // GROUP + 1,)),
             pltpu.SemaphoreType.DMA,
             pltpu.VMEM((3, 1, 128), jnp.float32),
             pltpu.VMEM((15, 1, 128), jnp.float32),
@@ -314,6 +325,10 @@
             pltpu.SemaphoreType.DMA,
             pltpu.SemaphoreType.REGULAR,
             pltpu.VMEM((8, width), jnp.float32),
+            pltpu.SMEM(token_counts.shape, jnp.int32),
+            pltpu.SMEM(flags.shape, jnp.int32),
+            pltpu.SemaphoreType.DMA,
+            pltpu.SemaphoreType.DMA,
         ],
         compiler_params=pltpu.CompilerParams(
             collective_id=0, has_side_effects=True, vmem_limit_bytes=56 << 20
@@ -322,36 +337,29 @@
 
 
 def update(grad, scale_hbm, param, first, second, *rest):
-    outs, held, bufs, scale, gsem, sems, ssem = rest[:4], rest[4:8], rest[8:12], *rest[12:]
-    step = bufs[0].shape[0] // STEPS
+    outs, held, kept, scale, gsem, sems, ssem = rest[:4], *rest[4:]
+    step = kept.shape[1] // STEPS
     get = pltpu.make_async_copy(scale_hbm, scale, ssem)
     get.start()
-    loads = []
-    for i in range(STEPS):
-        part = pl.ds(i * step, step)
+    parts = [pl.ds(i * step, step) for i in range(STEPS)]
+    for i, part in enumerate(parts):
         sources = (grad.at[part], param.at[0, part], first.at[0, part], second.at[0, part])
-        loads.append([])
         for j, source in enumerate(sources):
-            loads[i].append(pltpu.make_async_copy(source, held[j].at[part], gsem.at[j, i]))
-            loads[i][j].start()
+            pltpu.make_async_copy(source, held.at[j, part], gsem.at[i]).start()
     get.wait()
     unbias_one, unbias_two = scale[1:2, :], scale[2:3, :]
-    stores = []
-    for i in range(STEPS):
-        part = pl.ds(i * step, step)
-        for load in loads[i]:
-            load.wait()
-        clipped = held[0][part, :] * scale[0:1, :]
-        now = held[1][part, :]
-        one = beta_first * held[2][part, :] + (1.0 - beta_first) * clipped
-        two = beta_second * held[3][part, :] + (1.0 - beta_second) * clipped * clipped
+    for i, part in enumerate(parts):
+        pltpu.make_async_copy(held.at[:, part], held.at[:, part], gsem.at[i]).wait()
+        clipped = held[0, part, :] * scale[0:1, :]
+        now = held[1, part, :]
+        one = beta_first * held[2, part, :] + (1.0 - beta_first) * clipped
+        two = beta_second * held[3, part, :] + (1.0 - beta_second) * clipped * clipped
         turn = one * unbias_one / (jnp.sqrt(two * unbias_two) + adam_epsilon) + weight_decay * now
         for j, value in enumerate((now - learn_rate * turn, one, two, turn)):
-            bufs[j][part, :] = value
-            stores.append(pltpu.make_async_copy(bufs[j].at[part], outs[j].at[0, part], sems.at[j, i]))
-            stores[-1].start()
-    for store in stores:
-        store.wait()
+            kept[j, part, :] = value
+            pltpu.make_async_copy(kept.at[j, part], outs[j].at[0, part], sems.at[j]).start()
+    for j in range(4):
+        pltpu.make_async_copy(kept.at[j], outs[j].at[0], sems.at[j]).wait()
 
 
 def local(
@@ -373,10 +381,11 @@
         in_specs=(anywhere,) * 5,
         out_specs=(anywhere,) * 4,
         scratch_shapes=[
-            *[pltpu.VMEM((shard_rows, width), jnp.float32)] * 8,
+            pltpu.VMEM((4, shard_rows, width), jnp.float32),
+            pltpu.VMEM((4, shard_rows, width), jnp.float32),
             pltpu.VMEM((8, width), jnp.float32),
-            pltpu.SemaphoreType.DMA((4, STEPS)),
-            pltpu.SemaphoreType.DMA((4, STEPS)),
+            pltpu.SemaphoreType.DMA((STEPS,)),
+            pltpu.SemaphoreType.DMA((4,)),
             pltpu.SemaphoreType.DMA,
         ],
         compiler_params=pltpu.CompilerParams(vmem_limit_bytes=60 << 20),

time: 76 us -> 71 us (0.934)
  Pallas kernels: 75.2 us -> 70.2 us
    pallas_call x1, Pallas kernels: 72.1 us -> 67.3 us  [reduced(): pl.pallas_call(functools.partial(kernel, entries), out_shape=(jax.ShapeDt...]
where the time goes in v3:
time: 71 us; the launch traced here: 70.8 us
  Pallas kernels  70.2 us (99%)
    pallas_call x1, Pallas kernels, reduced(): pl.pallas_call(functools.partial(kernel, entries), out_shape=(jax.ShapeDt...  67.3 us
    pallas_call x1, Pallas kernels, local(): pl.pallas_call(update, out_shape=(jax.ShapeDtypeStruct(master_param.shape...  2.89 us

profile of v3, /device:TPU:1, one launch (start us, length us, event | category | flops | bytes accessed | tf_op | source)
XLA Modules:
  0.0 70.8 jit_solution(1014037282325641010)
XLA Ops:
  0.6 67.3 %shard_map.102 = (f32[256,512]{1,0:T(8,128)}, f32[8,512]{1,0:T(8,128)}) custom-call(bf16[1,480,8192]{2,1,0:T(8,128)(2,1)} %x_hbm.1, bf16[1,480,512]{2,1,0:T(8,128)(2,1)} %m_hbm.1, s32[1,4]{1,0:T(1,128)} %counts_hbm.1, s32[8]{0:T(128)} %flags_hbm.1), custom_call_target="tpu_custom_call" | custom-call | tf_op jit(solution)/shard_map/pallas_call | solution.py:291
  68.0 2.9 %shard_map.103 = (f32[1,256,512]{2,1,0:T(8,128)}, f32[1,256,512]{2,1,0:T(8,128)}, f32[1,256,512]{2,1,0:T(8,128)}, f32[1,256,512]{2,1,0:T(8,128)}) custom-call(f32[256,512]{1,0:T(8,128)} %get-tuple-element.6.grad, f32[8,512]{1,0:T(8,128)} %get-tuple-element.7.scale_hbm, f32[1,256,512]{2,1,0:T(8,128)} %param.15, f32[1,256,512]{2,1,0:T(8,128)} %first.1, ...), custom_call_target="tpu_custom_call" | custom-call | flops 2621440 | bytes 4194304 | tf_op jit(solution)/shard_map/pallas_call | solution.py:378

commit v4 on v3

--- a/solution.py
+++ b/solution.py
@@ -103,7 +103,7 @@
 
 def kernel(entries, x_hbm, m_hbm, counts_hbm, flags_hbm, g_out, scale_out, xbuf, mbuf, masked, mt, part, tmp, grad, *rest):
     snd, rcv, hsnd, hrcv = rest[0:4], rest[4:8], rest[8:12], rest[12:16]
-    ssem, rsem, hssem, dummy, xsem, msem, red, redr0, redr1, s0, r0, s1, r1, turned, gsem, far, scale, counts, flags, csem, fsem = rest[16:]
+    ssem, rsem, hssem, dummy, xsem, msem, red, heard, s0, r0, turned, gsem, far, scale, counts, flags, csem, fsem, kin = rest[16:]
     width = mbuf.shape[1]
     section, dp = lax.axis_index("section"), lax.axis_index("dp")
     y, core = section // 2, lax.rem(section, 2)
@@ -115,8 +115,16 @@
             "dp": lax.rem(z + dz + NZ, NZ) * NX + lax.rem(x + dx + NX, NX),
         }
 
-    plane = [(0, dx, dy, 0) for dx in range(NX) for dy in range(NY) if (dx, dy) != (0, 0)]
-    column = [(dz, 0, 0, dc) for dz in range(NZ) for dc in range(2) if (dz, dc) != (0, 0)]
+    offsets = [
+        (dz, dx, dy, dc) for dz in range(NZ) for dx in range(NX) for dy in range(NY) for dc in range(2)
+    ]
+    others = sorted(offsets[1:], key=lambda d: -sum(min(a, n - a) for a, n in zip(d, (NZ, NX, NY, 2))))
+
+    barrier = pltpu.get_barrier_semaphore()
+    peers = [(1, 0, 0, 0), (-1, 0, 0, 0), (0, 1, 0, 0), (0, -1, 0, 0)]
+    peers += [(0, 0, 1, 0), (0, 0, -1, 0), (0, 0, 0, 1)]
+    for peer in peers:
+        pl.semaphore_signal(barrier, inc=1, device_id=at(*peer), device_id_type=MESH)
 
     mload = pltpu.make_async_copy(m_hbm.at[0], mbuf, msem)
     mload.start()
@@ -131,12 +139,6 @@
         )
 
     xload(0).start()
-
-    barrier = pltpu.get_barrier_semaphore()
-    peers = [(1, 0, 0, 0), (-1, 0, 0, 0), (0, 1, 0, 0), (0, -1, 0, 0)]
-    peers += [(0, 0, 1, 0), (0, 0, -1, 0), (0, 0, 0, 1)]
-    for peer in peers:
-        pl.semaphore_signal(barrier, inc=1, device_id=at(*peer), device_id_type=MESH)
 
     fload = pltpu.make_async_copy(flags_hbm, flags, fsem)
     fload.start()
@@ -186,8 +188,11 @@
     sums = jnp.zeros((8, 256), jnp.float32)
     for place, name in enumerate(SEQUENCE):
         c, block, ins, out = TASKS[name]
+        if place == 12:
+            pl.semaphore_wait(far, 1)
+            pl.semaphore_signal(kin, inc=1, device_id=at(0, 0, 0, 1), device_id_type=MESH)
         if place == 24:
-            pl.semaphore_wait(far, 1)
+            pl.semaphore_wait(kin, 1)
         first, rows = PIECES[c]
         k, step = CLASSES.index(c), STEP[c]
         need(block)
@@ -244,27 +249,27 @@
         data.start()
 
     sums = jnp.sum(sums, axis=0, keepdims=True)
-    red[0] = sums[:, :128] + sums[:, 128:]
-    for q, (dirs, dst, ss, rs) in enumerate(((plane, redr0, s0, r0), (column, redr1, s1, r1))):
-        for j, d in enumerate(dirs):
+    red[...] = sums[:, :LANES] + sums[:, LANES:]
+    zs = [lax.rem(z + d, NZ) * NX for d in range(NZ)]
+    xs = [lax.rem(x + d, NX) for d in range(NX)]
+    ys = [lax.rem(y + d, NY) * 2 for d in range(NY)]
+    cs = [core, 1 - core]
+    for j, (dz, dx, dy, dc) in enumerate(others):
+        to = {"section": ys[dy] + cs[dc], "dp": zs[dz] + xs[dx]}
+        pltpu.make_async_remote_copy(red, heard.at[j], s0, r0, device_id=to, device_id_type=MESH).start()
+    for k in range(len(CLASSES)):
+        for buf, sem in ((snd[k], ssem.at[k]), (hsnd[k], hssem.at[k])):
             pltpu.make_async_remote_copy(
-                red.at[q], dst.at[j], ss, rs, device_id=at(*d), device_id_type=MESH
-            ).start()
-        if q == 0:
-            for k in range(len(CLASSES)):
-                for buf, sem in ((snd[k], ssem.at[k]), (hsnd[k], hssem.at[k])):
-                    pltpu.make_async_remote_copy(
-                        buf, buf, sem, rsem.at[0], device_id=at(dx=1), device_id_type=MESH
-                    ).wait_send()
-            for j in range(0, 256, 128):
-                turned[j : j + 128, :] = grad[:, j : j + 128].T
-            store = pltpu.make_async_copy(turned, g_out, gsem)
-            store.start()
-        whole = pltpu.make_async_remote_copy(dst, dst, ss, rs, device_id=at(*dirs[0]), device_id_type=MESH)
-        whole.wait_recv()
-        red[q + 1] = red[q] + jnp.sum(dst[...], axis=0)
-        whole.wait_send()
-    total_sq = jnp.sum(red[2], axis=1, keepdims=True)
+                buf, buf, sem, rsem.at[0], device_id=at(dx=1), device_id_type=MESH
+            ).wait_send()
+    for j in range(0, 256, 128):
+        turned[j : j + 128, :] = grad[:, j : j + 128].T
+    store = pltpu.make_async_copy(turned, g_out, gsem)
+    store.start()
+    whole = pltpu.make_async_remote_copy(heard, heard, s0, r0, device_id=at(dx=1), device_id_type=MESH)
+    whole.wait_recv()
+    total_sq = jnp.sum(red[...] + jnp.sum(heard[...], axis=0), axis=1, keepdims=True)
+    whole.wait_send()
     clip_scale = clip_level * math.sqrt(entries) / (jnp.sqrt(total_sq) + 1e-06)
     fload.wait()
     power_one, power_two = jnp.float32(beta_first), jnp.float32(beta_second)
@@ -314,11 +319,8 @@
             pltpu.VMEM((4 * 162, 1, LANES), jnp.float32),
             pltpu.SemaphoreType.DMA((len(BLOCKS) // GROUP + 1,)),
             pltpu.SemaphoreType.DMA,
-            pltpu.VMEM((3, 1, 128), jnp.float32),
-            pltpu.VMEM((15, 1, 128), jnp.float32),
-            pltpu.VMEM((15, 1, 128), jnp.float32),
-            pltpu.SemaphoreType.DMA,
-            pltpu.SemaphoreType.DMA,
+            pltpu.VMEM((1, LANES), jnp.float32),
+            pltpu.VMEM((255, 1, LANES), jnp.float32),
             pltpu.SemaphoreType.DMA,
             pltpu.SemaphoreType.DMA,
             pltpu.VMEM((256, width), jnp.float32),
@@ -329,6 +331,7 @@
             pltpu.SMEM(flags.shape, jnp.int32),
             pltpu.SemaphoreType.DMA,
             pltpu.SemaphoreType.DMA,
+            pltpu.SemaphoreType.REGULAR,
         ],
         compiler_params=pltpu.CompilerParams(
             collective_id=0, has_side_effects=True, vmem_limit_bytes=56 << 20

time: 71 us -> 69.1 us (0.973)
  Pallas kernels: 70.2 us -> 68.3 us
    pallas_call x1, Pallas kernels: 67.3 us -> 65.4 us  [reduced(): pl.pallas_call(functools.partial(kernel, entries), out_shape=(jax.ShapeDt...]
where the time goes in v4:
time: 69.1 us; the launch traced here: 69 us
  Pallas kernels  68.3 us (99%)
    pallas_call x1, Pallas kernels, reduced(): pl.pallas_call(functools.partial(kernel, entries), out_shape=(jax.ShapeDt...  65.4 us
    pallas_call x1, Pallas kernels, local(): pl.pallas_call(update, out_shape=(jax.ShapeDtypeStruct(master_param.shape...  2.89 us

profile of v4, /device:TPU:1, one launch (start us, length us, event | category | flops | bytes accessed | tf_op | source)
XLA Modules:
  0.0 69.0 jit_solution(1896570611825521436)
XLA Ops:
  0.6 65.4 %shard_map.102 = (f32[256,512]{1,0:T(8,128)}, f32[8,512]{1,0:T(8,128)}) custom-call(bf16[1,480,8192]{2,1,0:T(8,128)(2,1)} %x_hbm.1, bf16[1,480,512]{2,1,0:T(8,128)(2,1)} %m_hbm.1, s32[1,4]{1,0:T(1,128)} %counts_hbm.1, s32[8]{0:T(128)} %flags_hbm.1), custom_call_target="tpu_custom_call" | custom-call | tf_op jit(solution)/shard_map/pallas_call | solution.py:296
  66.1 2.9 %shard_map.103 = (f32[1,256,512]{2,1,0:T(8,128)}, f32[1,256,512]{2,1,0:T(8,128)}, f32[1,256,512]{2,1,0:T(8,128)}, f32[1,256,512]{2,1,0:T(8,128)}) custom-call(f32[256,512]{1,0:T(8,128)} %get-tuple-element.6.grad, f32[8,512]{1,0:T(8,128)} %get-tuple-element.7.scale_hbm, f32[1,256,512]{2,1,0:T(8,128)} %param.15, f32[1,256,512]{2,1,0:T(8,128)} %first.1, ...), custom_call_target="tpu_custom_call" | custom-call | flops 2621440 | bytes 4194304 | tf_op jit(solution)/shard_map/pallas_call | solution.py:381

commit v5 on v4

--- a/solution.py
+++ b/solution.py
@@ -25,28 +25,30 @@
 STEP = {"A0": 160, "A1": 144, "B0": 96, "B1": 112}
 DZ_ORDER = (4, 3, -3, 2, -2, 1, -1, 0)
 DX_ORDER = (2, 1, -1, 0)
+FLIP_Z, FLIP_X = (3, 2, 1), (1,)
 
 ORDER = (
-    0, 96, 64, 32, 8, 104, 80, 41, 72, 84, 9, 112, 36, 124, 108, 88,
-    68, 12, 120, 40, 17, 81, 49, 100, 16, 1, 76, 105, 97, 4, 65, 69,
-    89, 60, 73, 34, 113, 109, 2, 77, 56, 85, 33, 101, 92, 42, 44, 24,
-    116, 38, 10, 114, 5, 66, 52, 3, 98, 121, 6, 28, 125, 106, 82, 90,
-    37, 102, 48, 45, 115, 35, 18, 110, 46, 117, 13, 11, 14, 99, 67, 26,
-    7, 70, 83, 43, 50, 86, 20, 107, 39, 54, 122, 74, 25, 118, 103, 57,
-    53, 19, 21, 78, 15, 58, 51, 71, 47, 22, 61, 75, 111, 93, 126, 87,
-    62, 27, 91, 119, 123, 55, 30, 29, 59, 94, 79, 23, 127, 63, 31, 95,
+    96, 0, 32, 64, 80, 112, 4, 100, 36, 12, 44, 120, 116, 72, 40, 16,
+    8, 104, 84, 76, 97, 108, 1, 2, 88, 81, 68, 65, 92, 9, 117, 73,
+    34, 124, 33, 37, 101, 121, 13, 6, 48, 5, 98, 105, 38, 85, 113, 56,
+    3, 45, 14, 41, 66, 109, 69, 93, 77, 10, 28, 35, 99, 46, 102, 106,
+    82, 74, 7, 42, 67, 20, 18, 70, 24, 52, 114, 17, 89, 49, 39, 50,
+    11, 125, 60, 21, 25, 110, 43, 107, 22, 58, 115, 122, 118, 103, 78, 15,
+    19, 26, 86, 90, 47, 57, 83, 126, 54, 51, 71, 53, 75, 123, 61, 62,
+    23, 29, 30, 27, 119, 91, 111, 94, 59, 55, 87, 79, 127, 31, 95, 63,
 )
 
 
 def build_tasks():
     tasks = {}
     for c in ("A0", "A1"):
-        sg = SIGN[c]
         for dz in DZ_ORDER:
+            sg = -SIGN[c] if dz in FLIP_Z else SIGN[c]
             tasks[(c, "x", dz, 2 * sg)] = (c, (dz, 2), (), ("x", sg))
             tasks[(c, "x", dz, -sg)] = (c, (dz, -sg), (), ("x", -sg))
             tasks[(c, "x", dz, sg)] = (c, (dz, sg), ((c, "x", dz, 2 * sg),), ("x", sg))
             ins = [(c, "x", dz, sg), (c, "x", dz, -sg)]
+            sg = SIGN[c]
             d = dz if dz != 4 else 4 * sg
             out = None
             if d == 0:
@@ -58,8 +60,8 @@
                 out = ("z", s)
             tasks[(c, "z", d)] = (c, (dz, 0), tuple(ins), out)
     for c in ("B0", "B1"):
-        sg = SIGN[c]
         for dx in DX_ORDER:
+            sg = -SIGN[c] if dx in FLIP_X else SIGN[c]
             for k in (4, 3, 2, 1):
                 d = k * sg
                 ins = () if k == 4 else ((c, "z", dx, d + sg),)
@@ -69,6 +71,7 @@
                 ins = () if k == 3 else ((c, "z", dx, d - sg),)
                 tasks[(c, "z", dx, d)] = (c, (d, dx), ins, ("z", -sg))
             ins = [(c, "z", dx, sg), (c, "z", dx, -sg)]
+            sg = SIGN[c]
             out, d = None, dx
             if dx == 0:
                 ins += [(c, "x", sg), (c, "x", -sg)]
@@ -101,7 +104,7 @@
 STEPS = 4
 
 
-def kernel(entries, x_hbm, m_hbm, counts_hbm, flags_hbm, g_out, scale_out, xbuf, mbuf, masked, mt, part, tmp, grad, *rest):
+def kernel(x_hbm, m_hbm, counts_hbm, flags_hbm, g_out, scale_out, xbuf, mbuf, masked, mt, part, tmp, grad, *rest):
     snd, rcv, hsnd, hrcv = rest[0:4], rest[4:8], rest[8:12], rest[12:16]
     ssem, rsem, hssem, dummy, xsem, msem, red, heard, s0, r0, turned, gsem, far, scale, counts, flags, csem, fsem, kin = rest[16:]
     width = mbuf.shape[1]
@@ -188,10 +191,10 @@
     sums = jnp.zeros((8, 256), jnp.float32)
     for place, name in enumerate(SEQUENCE):
         c, block, ins, out = TASKS[name]
-        if place == 12:
+        if place == 10:
             pl.semaphore_wait(far, 1)
             pl.semaphore_signal(kin, inc=1, device_id=at(0, 0, 0, 1), device_id_type=MESH)
-        if place == 24:
+        if place == 20:
             pl.semaphore_wait(kin, 1)
         first, rows = PIECES[c]
         k, step = CLASSES.index(c), STEP[c]
@@ -199,12 +202,12 @@
         b = BLOCKS.index(block)
         scales = []
         if ins:
-            whole = dummy.at[pl.ds(0, len(ins) * (rows + 2))]
+            whole = dummy.at[pl.ds(0, len(ins) * (rows + 1))]
             pltpu.make_async_remote_copy(
                 whole, whole, ssem.at[k], rsem.at[TAKER[ins[0]]], device_id=at(dx=1), device_id_type=MESH
             ).wait_recv()
         for n in ins:
-            scales.append(hrcv[k][MESSAGES[n][1]])
+            scales.append(jnp.concatenate([hrcv[k][MESSAGES[n][1]]] * 2, axis=1))
 
         def value(r, size):
             acc = part[b, pl.ds(first + r, size), :]
@@ -229,10 +232,10 @@
             return jnp.maximum(top, jnp.max(jnp.abs(acc).reshape(step // 8, 8, 256), axis=0))
 
         top = lax.fori_loop(0, rows // step, high, jnp.full((8, 256), TINY, jnp.float32))
-        top = jnp.max(top, axis=0, keepdims=True)
+        top = jnp.max(jnp.maximum(top[:, :LANES], top[:, LANES:]), axis=0, keepdims=True)
         i = MESSAGES[name][1]
         hsnd[k][i] = top * (1.0 / LIMIT)
-        inverse = LIMIT / top
+        inverse = jnp.concatenate([LIMIT / top] * 2, axis=1)
 
         def narrow(g, _):
             acc = tmp[pl.ds(g * step, step), :] if ins else part[b, pl.ds(first + g * step, step), :]
@@ -267,10 +270,6 @@
     store = pltpu.make_async_copy(turned, g_out, gsem)
     store.start()
     whole = pltpu.make_async_remote_copy(heard, heard, s0, r0, device_id=at(dx=1), device_id_type=MESH)
-    whole.wait_recv()
-    total_sq = jnp.sum(red[...] + jnp.sum(heard[...], axis=0), axis=1, keepdims=True)
-    whole.wait_send()
-    clip_scale = clip_level * math.sqrt(entries) / (jnp.sqrt(total_sq) + 1e-06)
     fload.wait()
     power_one, power_two = jnp.float32(beta_first), jnp.float32(beta_second)
     for i in range(flags.shape[0]):
@@ -278,23 +277,26 @@
         power_one = power_one * jnp.where(counted, jnp.float32(beta_first), jnp.float32(1.0))
         power_two = power_two * jnp.where(counted, jnp.float32(beta_second), jnp.float32(1.0))
     shape = (1, width)
-    scale[0:1, :] = jnp.broadcast_to(clip_scale, shape)
     scale[1:2, :] = 1.0 / (1.0 - jnp.full(shape, power_one, jnp.float32))
     scale[2:3, :] = 1.0 / (1.0 - jnp.full(shape, power_two, jnp.float32))
     scale[3:8, :] = jnp.zeros((5, width), jnp.float32)
+    scale[0:1, LANES:] = jnp.zeros((1, width - LANES), jnp.float32)
+    whole.wait_recv()
+    scale[0:1, :LANES] = red[...] + jnp.sum(heard[...], axis=0)
     put = pltpu.make_async_copy(scale, scale_out, msem)
     put.start()
+    whole.wait_send()
     put.wait()
     store.wait()
 
 
-def reduced(layer_inputs, key_cotangent, token_counts, flags, entries):
+def reduced(layer_inputs, key_cotangent, token_counts, flags):
     _, tokens, depth = layer_inputs.shape
     width = key_cotangent.shape[2]
     anywhere = pl.BlockSpec(memory_space=pltpu.HBM)
     pieces = [PIECES[c][1] for c in CLASSES]
     return pl.pallas_call(
-        functools.partial(kernel, entries),
+        kernel,
         out_shape=(
             jax.ShapeDtypeStruct((256, width), jnp.float32),
             jax.ShapeDtypeStruct((8, width), jnp.float32),
@@ -311,12 +313,12 @@
             pltpu.VMEM((width, 256), jnp.float32),
             *[pltpu.VMEM((N_MSG, r, 256), jnp.int16) for r in pieces],
             *[pltpu.VMEM((N_MSG, r, 256), jnp.int16) for r in pieces],
-            *[pltpu.VMEM((N_MSG, 1, 256), jnp.float32) for r in pieces],
-            *[pltpu.VMEM((N_MSG, 1, 256), jnp.float32) for r in pieces],
+            *[pltpu.VMEM((N_MSG, 1, LANES), jnp.float32) for r in pieces],
+            *[pltpu.VMEM((N_MSG, 1, LANES), jnp.float32) for r in pieces],
             pltpu.SemaphoreType.DMA((len(CLASSES),)),
             pltpu.SemaphoreType.DMA((len(TAKERS),)),
             pltpu.SemaphoreType.DMA((len(CLASSES),)),
-            pltpu.VMEM((4 * 162, 1, LANES), jnp.float32),
+            pltpu.VMEM((4 * 161, 1, LANES), jnp.float32),
             pltpu.SemaphoreType.DMA((len(BLOCKS) // GROUP + 1,)),
             pltpu.SemaphoreType.DMA,
             pltpu.VMEM((1, LANES), jnp.float32),
@@ -339,7 +341,7 @@
     )(layer_inputs, key_cotangent, token_counts, flags)
 
 
-def update(grad, scale_hbm, param, first, second, *rest):
+def update(entries, grad, scale_hbm, param, first, second, *rest):
     outs, held, kept, scale, gsem, sems, ssem = rest[:4], *rest[4:]
     step = kept.shape[1] // STEPS
     get = pltpu.make_async_copy(scale_hbm, scale, ssem)
@@ -351,9 +353,12 @@
             pltpu.make_async_copy(source, held.at[j, part], gsem.at[i]).start()
     get.wait()
     unbias_one, unbias_two = scale[1:2, :], scale[2:3, :]
+    total_sq = jnp.sum(scale[0:1, :], axis=1, keepdims=True)
+    clip_scale = clip_level * math.sqrt(entries) / (jnp.sqrt(total_sq) + 1e-06)
+    clip_scale = jnp.broadcast_to(clip_scale, unbias_one.shape)
     for i, part in enumerate(parts):
         pltpu.make_async_copy(held.at[:, part], held.at[:, part], gsem.at[i]).wait()
-        clipped = held[0, part, :] * scale[0:1, :]
+        clipped = held[0, part, :] * clip_scale
         now = held[1, part, :]
         one = beta_first * held[2, part, :] + (1.0 - beta_first) * clipped
         two = beta_second * held[3, part, :] + (1.0 - beta_second) * clipped * clipped
@@ -376,10 +381,10 @@
 ):
     _, shard_rows, width = master_param.shape
     entries = lax.axis_size("section") * lax.axis_size("dp") * shard_rows * width
-    gradient, scale = reduced(layer_inputs, key_cotangent, token_counts, rollback_flags, entries)
+    gradient, scale = reduced(layer_inputs, key_cotangent, token_counts, rollback_flags)
     anywhere = pl.BlockSpec(memory_space=pltpu.HBM)
     return pl.pallas_call(
-        update,
+        functools.partial(update, entries),
         out_shape=(jax.ShapeDtypeStruct(master_param.shape, jnp.float32),) * 4,
         in_specs=(anywhere,) * 5,
         out_specs=(anywhere,) * 4,

time: 69.1 us -> 68.6 us (level)
  no operation moved by 1% of the time
where the time goes in v5:
time: 68.6 us; the launch traced here: 68.5 us
  Pallas kernels  67.8 us (99%)
    pallas_call x1, Pallas kernels, reduced(): pl.pallas_call(kernel, out_shape=(jax.ShapeDtypeStruct((256, width), jnp....  64.8 us
    pallas_call x1, Pallas kernels, local(): pl.pallas_call(functools.partial(update, entries), out_shape=(jax.ShapeDt...  2.99 us

profile of v5, /device:TPU:1, one launch (start us, length us, event | category | flops | bytes accessed | tf_op | source)
XLA Modules:
  0.0 68.5 jit_solution(9783424830489747671)
XLA Ops:
  0.6 64.8 %shard_map.102 = (f32[256,512]{1,0:T(8,128)}, f32[8,512]{1,0:T(8,128)}) custom-call(bf16[1,480,8192]{2,1,0:T(8,128)(2,1)} %x_hbm.1, bf16[1,480,512]{2,1,0:T(8,128)(2,1)} %m_hbm.1, s32[1,4]{1,0:T(1,128)} %counts_hbm.1, s32[8]{0:T(128)} %flags_hbm.1), custom_call_target="tpu_custom_call" | custom-call | tf_op jit(solution)/shard_map/pallas_call | solution.py:298
  65.5 3.0 %shard_map.103 = (f32[1,256,512]{2,1,0:T(8,128)}, f32[1,256,512]{2,1,0:T(8,128)}, f32[1,256,512]{2,1,0:T(8,128)}, f32[1,256,512]{2,1,0:T(8,128)}) custom-call(f32[256,512]{1,0:T(8,128)} %get-tuple-element.6.grad, f32[8,512]{1,0:T(8,128)} %get-tuple-element.7.scale_hbm, f32[1,256,512]{2,1,0:T(8,128)} %param.15, f32[1,256,512]{2,1,0:T(8,128)} %first.1, ...), custom_call_target="tpu_custom_call" | custom-call | flops 2621440 | bytes 4194304 | tf_op jit(solution)/shard_map/pallas_call | solution.py:386

commit v6 on v5

--- a/solution.py
+++ b/solution.py
@@ -96,7 +96,13 @@
         _c = TASKS[_n][0]
         MESSAGES[_n] = (_c, sum(1 for m in MESSAGES if MESSAGES[m][0] == _c))
 TAKERS = [n for n in SEQUENCE if TASKS[n][2]]
-TAKER = {m: i for i, n in enumerate(TAKERS) for m in TASKS[n][2]}
+SLOT = (
+    0, 1, 2, 3, 4, 5, 6, 7, 8, 9, 10, 11, 12, 13, 14, 15, 16, 17, 18, 19,
+    20, 21, 22, 23, 24, 25, 26, 0, 27, 28, 29, 30, 31, 32, 1, 33, 34, 35, 36, 37,
+    38, 2, 39, 3, 4, 40, 5, 41, 42, 43, 44, 45, 6, 7, 46, 8, 47, 9, 10, 48,
+    49, 50, 11, 0, 12, 51, 52, 13, 14, 1, 15, 53, 16, 17, 18, 19, 20, 21, 2, 22,
+)
+TAKER = {m: SLOT[i] for i, n in enumerate(TAKERS) for m in TASKS[n][2]}
 N_MSG = 31
 CLASSES = ("A0", "A1", "B0", "B1")
 LANES = 128
@@ -316,7 +322,7 @@
             *[pltpu.VMEM((N_MSG, 1, LANES), jnp.float32) for r in pieces],
             *[pltpu.VMEM((N_MSG, 1, LANES), jnp.float32) for r in pieces],
             pltpu.SemaphoreType.DMA((len(CLASSES),)),
-            pltpu.SemaphoreType.DMA((len(TAKERS),)),
+            pltpu.SemaphoreType.DMA((max(SLOT) + 1,)),
             pltpu.SemaphoreType.DMA((len(CLASSES),)),
             pltpu.VMEM((4 * 161, 1, LANES), jnp.float32),
             pltpu.SemaphoreType.DMA((len(BLOCKS) // GROUP + 1,)),

time: 68.6 us -> 68.4 us (level)
  no operation moved by 1% of the time
where the time goes in v6:
time: 68.4 us; the launch traced here: 68.2 us
  Pallas kernels  67.6 us (99%)
    pallas_call x1, Pallas kernels, reduced(): pl.pallas_call(kernel, out_shape=(jax.ShapeDtypeStruct((256, width), jnp....  64.6 us
    pallas_call x1, Pallas kernels, local(): pl.pallas_call(functools.partial(update, entries), out_shape=(jax.ShapeDt...  2.99 us

profile of v6, /device:TPU:1, one launch (start us, length us, event | category | flops | bytes accessed | tf_op | source)
XLA Modules:
  0.0 68.2 jit_solution(15546682225551612834)
XLA Ops:
  0.6 64.6 %shard_map.102 = (f32[256,512]{1,0:T(8,128)}, f32[8,512]{1,0:T(8,128)}) custom-call(bf16[1,480,8192]{2,1,0:T(8,128)(2,1)} %x_hbm.1, bf16[1,480,512]{2,1,0:T(8,128)(2,1)} %m_hbm.1, s32[1,4]{1,0:T(1,128)} %counts_hbm.1, s32[8]{0:T(128)} %flags_hbm.1), custom_call_target="tpu_custom_call" | custom-call | tf_op jit(solution)/shard_map/pallas_call | solution.py:304
  65.2 3.0 %shard_map.103 = (f32[1,256,512]{2,1,0:T(8,128)}, f32[1,256,512]{2,1,0:T(8,128)}, f32[1,256,512]{2,1,0:T(8,128)}, f32[1,256,512]{2,1,0:T(8,128)}) custom-call(f32[256,512]{1,0:T(8,128)} %get-tuple-element.6.grad, f32[8,512]{1,0:T(8,128)} %get-tuple-element.7.scale_hbm, f32[1,256,512]{2,1,0:T(8,128)} %param.15, f32[1,256,512]{2,1,0:T(8,128)} %first.1, ...), custom_call_target="tpu_custom_call" | custom-call | flops 2621440 | bytes 4194304 | tf_op jit(solution)/shard_map/pallas_call | solution.py:392
